TPU v7x, 256 devices: a whole 4x4x8 slice. The times are simulated.
256 devices in a mesh: loop: 64 (over x_lo, z, y), team: 4 (over x_hi, core).
Axes of the slice: x: 4 (x_hi: 2, x_lo: 2; x = x_hi * 2 + x_lo), y: 4, z: 8, core: 2. Of those that a mesh axis runs over, the one named last changes fastest.
Arguments:
- samples: bfloat16 [4096, 11776], P(('loop', 'team')), may hold values from -6 to 6
- input_gains: float32 [2, 4096, 4, 128], P(None, 'loop', None, 'team'), may hold values from -5 to 5
Outputs:
- visibility: float32 [64, 4, 2, 256, 4096], P('loop', 'team')
All inputs are finite; a program needn't handle non-finite values.
Results may differ from a plain program's by a relative error of at most 0.0038.
Values may be sent and summed in bfloat16 or wider, within the bound.
No kernel may reach another device: no remote copies, remote signals or barrier semaphores. Data moves between devices by JAX's collectives and lax.ppermute only.
A program may use at most 64 MiB of HBM per device.

v0:
```python
import math
import jax
import jax.numpy as jnp
from jax import lax
from jax.sharding import PartitionSpec as P

FCH = 512
TAPS = 8
AVG = 32
SPEC = 16


def shifted(array, axis, by):
    count = lax.axis_size(axis)
    pairs = [(i, i + by) for i in range(count) if 0 <= i + by < count]
    return lax.ppermute(array, axis, pairs)


def from_behind(block, axis, distance):
    devices = range(lax.axis_size(axis))
    route = [((i - distance) % len(devices), i) for i in devices]
    return lax.ppermute(block, axis, route)


def pfb_window():
    sample_pos = jnp.arange(TAPS * FCH, dtype=jnp.float32) + 0.5
    taper = jnp.sin(jnp.pi * sample_pos / (TAPS * FCH)) ** 2
    taps_table = jnp.sinc(sample_pos / FCH - TAPS / 2) * taper
    return taps_table.reshape(TAPS, FCH)


def filter_bank(raw_rows, channel_index):
    rows_here = raw_rows.shape[0]
    frames = raw_rows.astype(jnp.float32).reshape(rows_here, SPEC + TAPS - 1, FCH)
    window = pfb_window()
    filtered = window[0] * frames[:, 0:SPEC, :]
    for tap_index in range(1, TAPS):
        filtered = filtered + window[tap_index] * frames[:, tap_index : tap_index + SPEC, :]
    channel_flat = channel_index.reshape(channel_index.shape[0], -1)
    positions = jnp.arange(FCH, dtype=jnp.int32)
    angles_table = (positions[:, None, None] * channel_flat[None] % FCH).astype(jnp.float32) * (
        2.0 * math.pi / FCH
    )
    dft_table = jnp.concatenate(
        [jnp.cos(angles_table), -jnp.sin(angles_table)], axis=2
    ) / math.sqrt(FCH)
    return jnp.einsum(
        "itp,pmc->imtc",
        filtered,
        dft_table,
        precision=lax.Precision.HIGHEST,
        preferred_element_type=jnp.float32,
    )


def apply_gains(spectra, gain_rows):
    rows_here = spectra.shape[0]
    bin_groups = gain_rows.shape[2]
    shaped = spectra.reshape(rows_here, SPEC, 2, bin_groups, AVG)
    real_part = shaped[:, :, 0]
    imag_part = shaped[:, :, 1]
    gain_re = gain_rows[0][:, None]
    gain_im = gain_rows[1][:, None]
    volt_re = (gain_re * real_part - gain_im * imag_part).astype(jnp.bfloat16)
    volt_im = (gain_re * imag_part + gain_im * real_part).astype(jnp.bfloat16)
    stacked = jnp.stack([volt_re, volt_im], axis=1)
    return stacked.transpose(3, 0, 1, 2, 4).reshape(bin_groups, rows_here, 2 * SPEC * AVG)


def local(samples, input_gains):
    member = lax.axis_index("team")
    team_size = lax.axis_size("team")
    loop_size = lax.axis_size("loop")
    loop_place = lax.axis_index("loop")
    team_rows = input_gains.shape[1]
    bin_groups = input_gains.shape[2]
    group_count = loop_size // bin_groups
    bin_slot = loop_place % bin_groups
    row_group = loop_place // bin_groups
    bin_range = jnp.arange(bin_groups, dtype=jnp.int32)
    avg_range = jnp.arange(AVG, dtype=jnp.int32)
    own_channels = (bin_range[:, None] * team_size + member) * AVG + avg_range[None, :]
    spectra = filter_bank(lax.all_gather(samples, "team", axis=0, tiled=True), own_channels[None])[
        :, 0
    ]
    packed_all = apply_gains(spectra, input_gains)
    width_k = packed_all.shape[2]
    own_part = lax.dynamic_index_in_dim(packed_all, bin_slot, 0, keepdims=False)
    gathered = jnp.zeros((bin_groups, team_rows, width_k), jnp.bfloat16)
    gathered = lax.dynamic_update_index_in_dim(gathered, own_part, bin_slot, 0)
    offsets = [value for value in range(1 - bin_groups, bin_groups) if value != 0]
    for row_offset in offsets:
        send_slot = jnp.clip(bin_slot + row_offset, 0, bin_groups - 1)
        outgoing = lax.dynamic_index_in_dim(packed_all, send_slot, 0, keepdims=False)
        incoming = shifted(outgoing, "loop", row_offset)
        anchor_slot = bin_slot - row_offset
        from_group = (anchor_slot >= 0) & (anchor_slot < bin_groups)
        store_slot = jnp.clip(anchor_slot, 0, bin_groups - 1)
        kept_rows = lax.dynamic_index_in_dim(gathered, store_slot, 0, keepdims=False)
        gathered = lax.dynamic_update_index_in_dim(
            gathered, jnp.where(from_group, incoming, kept_rows), store_slot, 0
        )
    rows_block = gathered.reshape(bin_groups * team_rows, width_k)
    width_rows = rows_block.shape[0]
    half_width = width_k // 2
    rotated = jnp.concatenate([rows_block[:, half_width:], -rows_block[:, :half_width]], axis=1)
    local_pair = jnp.stack([rows_block, rotated])
    norm_scale = 1.0 / (AVG * SPEC)
    nought = jnp.zeros((), jnp.int32)

    def place_tile(tile_state, partner, source_group):
        tile_values = (
            jnp.einsum("crk,pk->crp", local_pair, partner, preferred_element_type=jnp.float32)
            * norm_scale
        )
        start_col = source_group * width_rows
        return lax.dynamic_update_slice(tile_state, tile_values, (nought, nought, start_col))

    visibility = jnp.zeros((2, width_rows, width_rows * group_count), jnp.float32)
    visibility = place_tile(visibility, rows_block, row_group)

    def visit(visit_index, carry):
        partner, tile_state = carry
        partner = from_behind(partner, "loop", bin_groups)
        return (partner, place_tile(tile_state, partner, (row_group - visit_index) % group_count))

    partner, visibility = lax.fori_loop(1, group_count, visit, (rows_block, visibility))
    return visibility[None, None]


def solution(mesh):
    placed = (P(("loop", "team"), None), P(None, "loop", None, "team"))
    return jax.shard_map(
        local,
        mesh=mesh,
        in_specs=placed,
        out_specs=P("loop", "team", None, None, None),
        check_vma=False,
    )
```

profile of v0, /device:TPU:26, one launch (start us, length us, event | category | flops | bytes accessed | tf_op | source)
XLA Modules:
  0.0 318.6 jit_solution(12989422514897380619)
XLA Ops:
  9.1 1.8 fusion.26
  10.9 26.0 %all-gather.2.cloned.1.call-done = bf16[64,11776]{1,0:T(8,128)(2,1)} async-done(((bf16[16,11776]{1,0:T(8,128)(2,1)}), bf16[64,11776]{1,0:T(8,128)(2,1)}) %all-gather.2.cloned.1.call-update) | async-done | bytes 1507344 | tf_op jit(solution)/shard_map/all_gather | solution.py:83
  36.9 2.7 reshape.165
  39.6 2.8 fusion.2
  42.3 2.7 fusion.11
  47.4 2.4 collective-permute-start.1
  49.8 8.0 %collective-permute-start.2 = (bf16[64,1024]{1,0:T(8,128)(2,1)S(1)}, bf16[64,1024]{1,0:T(8,128)(2,1)S(1)}, u32[]{:S(2)}, u32[]{:S(2)}) collective-permute-start(bf16[64,1024]{1,0:T(8,128)(2,1)S(1)} %bitcast.98), channel_id=1, source_target_pairs={{8,0},{12,4},{16,8},{20,12},{24,16},{28,20},{32,24},{36,28},{40,32... | collective-permute-start | bytes 393224 | tf_op jit(solution)/shard_map/ppermute | solution.py:16
  57.8 1.9 collective-permute-start.3
  59.7 6.0 %collective-permute-start.4 = (bf16[64,1024]{1,0:T(8,128)(2,1)S(1)}, bf16[64,1024]{1,0:T(8,128)(2,1)S(1)}, u32[]{:S(2)}, u32[]{:S(2)}) collective-permute-start(bf16[64,1024]{1,0:T(8,128)(2,1)S(1)} %bitcast.96), channel_id=1, source_target_pairs={{0,4},{4,8},{8,12},{12,16},{16,20},{20,24},{24,28},{28,32},{32,36}... | collective-permute-start | bytes 393224 | tf_op jit(solution)/shard_map/ppermute | solution.py:16
  65.9 1.9 collective-permute-start.5
  67.9 1.9 collective-permute-start.6
  70.1 4.3 %collective-permute-done.5 = bf16[64,1024]{1,0:T(8,128)(2,1)S(1)} collective-permute-done((bf16[64,1024]{1,0:T(8,128)(2,1)S(1)}, bf16[64,1024]{1,0:T(8,128)(2,1)S(1)}, u32[]{:S(2)}, u32[]{:S(2)}) %collective-permute-start.5) | collective-permute-done | bytes 131104 | tf_op jit(solution)/shard_map/ppermute | solution.py:16
  74.4 2.5 collective-permute-done.6
  78.7 3.4 %copy-done = f32[2,256,4096]{2,1,0:T(8,128)} copy-done((f32[2,256,4096]{2,1,0:T(8,128)}, f32[2,256,4096]{2,1,0:T(8,128)S(1)}, u32[]{:S(2)}) %copy-start) | copy-done | bytes 8388632
  82.1 229.7 %while.17 = (s32[]{:T(128)}, bf16[256,1024]{1,0:T(8,128)(2,1)S(1)}, f32[2,256,4096]{2,1,0:T(8,128)}, bf16[2,256,1024]{2,1,0:T(8,128)(2,1)S(1)}, s32[]{:T(128)}, ...) while((s32[]{:T(128)}, bf16[256,1024]{1,0:T(8,128)(2,1)S(1)}, ...), condition=%wide.region_1.2_spmd, body=%wide.region_0.1_spmd.sunk | while | flops 268566560 | bytes 5243200 | solution.py:127
  82.1 15.5 %collective-permute-done = bf16[256,1024]{1,0:T(8,128)(2,1)S(1)} collective-permute-done((bf16[256,1024]{1,0:T(8,128)(2,1)S(1)}, bf16[256,1024]{1,0:T(8,128)(2,1)S(1)}, u32[]{:S(2)}, u32[]{:S(2)}) %collective-permute-start) | collective-permute-done | bytes 524320 | tf_op jit(solution)/shard_map/while/body/eval_jaxpr/ppermute | solution.py:22
  97.7 1.3 fusion.51
  98.9 14.6 %collective-permute-done = bf16[256,1024]{1,0:T(8,128)(2,1)S(1)} collective-permute-done((bf16[256,1024]{1,0:T(8,128)(2,1)S(1)}, bf16[256,1024]{1,0:T(8,128)(2,1)S(1)}, u32[]{:S(2)}, u32[]{:S(2)}) %collective-permute-start) | collective-permute-done | bytes 524320 | tf_op jit(solution)/shard_map/while/body/eval_jaxpr/ppermute | solution.py:22
  114.8 13.7 %collective-permute-done = bf16[256,1024]{1,0:T(8,128)(2,1)S(1)} collective-permute-done((bf16[256,1024]{1,0:T(8,128)(2,1)S(1)}, bf16[256,1024]{1,0:T(8,128)(2,1)S(1)}, u32[]{:S(2)}, u32[]{:S(2)}) %collective-permute-start) | collective-permute-done | bytes 524320 | tf_op jit(solution)/shard_map/while/body/eval_jaxpr/ppermute | solution.py:22
  129.8 12.7 %collective-permute-done = bf16[256,1024]{1,0:T(8,128)(2,1)S(1)} collective-permute-done((bf16[256,1024]{1,0:T(8,128)(2,1)S(1)}, bf16[256,1024]{1,0:T(8,128)(2,1)S(1)}, u32[]{:S(2)}, u32[]{:S(2)}) %collective-permute-start) | collective-permute-done | bytes 524320 | tf_op jit(solution)/shard_map/while/body/eval_jaxpr/ppermute | solution.py:22
  143.9 11.8 %collective-permute-done = bf16[256,1024]{1,0:T(8,128)(2,1)S(1)} collective-permute-done((bf16[256,1024]{1,0:T(8,128)(2,1)S(1)}, bf16[256,1024]{1,0:T(8,128)(2,1)S(1)}, u32[]{:S(2)}, u32[]{:S(2)}) %collective-permute-start) | collective-permute-done | bytes 524320 | tf_op jit(solution)/shard_map/while/body/eval_jaxpr/ppermute | solution.py:22
  157.0 11.4 %collective-permute-done = bf16[256,1024]{1,0:T(8,128)(2,1)S(1)} collective-permute-done((bf16[256,1024]{1,0:T(8,128)(2,1)S(1)}, bf16[256,1024]{1,0:T(8,128)(2,1)S(1)}, u32[]{:S(2)}, u32[]{:S(2)}) %collective-permute-start) | collective-permute-done | bytes 524320 | tf_op jit(solution)/shard_map/while/body/eval_jaxpr/ppermute | solution.py:22
  169.7 12.5 %collective-permute-done = bf16[256,1024]{1,0:T(8,128)(2,1)S(1)} collective-permute-done((bf16[256,1024]{1,0:T(8,128)(2,1)S(1)}, bf16[256,1024]{1,0:T(8,128)(2,1)S(1)}, u32[]{:S(2)}, u32[]{:S(2)}) %collective-permute-start) | collective-permute-done | bytes 524320 | tf_op jit(solution)/shard_map/while/body/eval_jaxpr/ppermute | solution.py:22
  183.5 13.6 %collective-permute-done = bf16[256,1024]{1,0:T(8,128)(2,1)S(1)} collective-permute-done((bf16[256,1024]{1,0:T(8,128)(2,1)S(1)}, bf16[256,1024]{1,0:T(8,128)(2,1)S(1)}, u32[]{:S(2)}, u32[]{:S(2)}) %collective-permute-start) | collective-permute-done | bytes 524320 | tf_op jit(solution)/shard_map/while/body/eval_jaxpr/ppermute | solution.py:22
  198.4 14.6 %collective-permute-done = bf16[256,1024]{1,0:T(8,128)(2,1)S(1)} collective-permute-done((bf16[256,1024]{1,0:T(8,128)(2,1)S(1)}, bf16[256,1024]{1,0:T(8,128)(2,1)S(1)}, u32[]{:S(2)}, u32[]{:S(2)}) %collective-permute-start) | collective-permute-done | bytes 524320 | tf_op jit(solution)/shard_map/while/body/eval_jaxpr/ppermute | solution.py:22
  214.3 15.8 %collective-permute-done = bf16[256,1024]{1,0:T(8,128)(2,1)S(1)} collective-permute-done((bf16[256,1024]{1,0:T(8,128)(2,1)S(1)}, bf16[256,1024]{1,0:T(8,128)(2,1)S(1)}, u32[]{:S(2)}, u32[]{:S(2)}) %collective-permute-start) | collective-permute-done | bytes 524320 | tf_op jit(solution)/shard_map/while/body/eval_jaxpr/ppermute | solution.py:22
  231.4 16.9 %collective-permute-done = bf16[256,1024]{1,0:T(8,128)(2,1)S(1)} collective-permute-done((bf16[256,1024]{1,0:T(8,128)(2,1)S(1)}, bf16[256,1024]{1,0:T(8,128)(2,1)S(1)}, u32[]{:S(2)}, u32[]{:S(2)}) %collective-permute-start) | collective-permute-done | bytes 524320 | tf_op jit(solution)/shard_map/while/body/eval_jaxpr/ppermute | solution.py:22
  249.6 16.0 %collective-permute-done = bf16[256,1024]{1,0:T(8,128)(2,1)S(1)} collective-permute-done((bf16[256,1024]{1,0:T(8,128)(2,1)S(1)}, bf16[256,1024]{1,0:T(8,128)(2,1)S(1)}, u32[]{:S(2)}, u32[]{:S(2)}) %collective-permute-start) | collective-permute-done | bytes 524320 | tf_op jit(solution)/shard_map/while/body/eval_jaxpr/ppermute | solution.py:22
  265.7 1.3 fusion.51
  267.0 15.2 %collective-permute-done = bf16[256,1024]{1,0:T(8,128)(2,1)S(1)} collective-permute-done((bf16[256,1024]{1,0:T(8,128)(2,1)S(1)}, bf16[256,1024]{1,0:T(8,128)(2,1)S(1)}, u32[]{:S(2)}, u32[]{:S(2)}) %collective-permute-start) | collective-permute-done | bytes 524320 | tf_op jit(solution)/shard_map/while/body/eval_jaxpr/ppermute | solution.py:22
  283.5 14.3 %collective-permute-done = bf16[256,1024]{1,0:T(8,128)(2,1)S(1)} collective-permute-done((bf16[256,1024]{1,0:T(8,128)(2,1)S(1)}, bf16[256,1024]{1,0:T(8,128)(2,1)S(1)}, u32[]{:S(2)}, u32[]{:S(2)}) %collective-permute-start) | collective-permute-done | bytes 524320 | tf_op jit(solution)/shard_map/while/body/eval_jaxpr/ppermute | solution.py:22
  299.1 11.3 %collective-permute-done = bf16[256,1024]{1,0:T(8,128)(2,1)S(1)} collective-permute-done((bf16[256,1024]{1,0:T(8,128)(2,1)S(1)}, bf16[256,1024]{1,0:T(8,128)(2,1)S(1)}, u32[]{:S(2)}, u32[]{:S(2)}) %collective-permute-start) | collective-permute-done | bytes 524320 | tf_op jit(solution)/shard_map/while/body/eval_jaxpr/ppermute | solution.py:22
  (89 shorter events, 24.0 us)
Async XLA Ops:
  6.5 30.3 %all-gather.2.cloned.1.call-start = ((), (), s32[]{:S(2)}) async-start(), calls=%async_computation | async-start | bytes 1884160 | tf_op jit(solution)/shard_map/all_gather | solution.py:83
  39.5 2.8 copy-start.1
  47.4 20.4 %collective-permute-start.1 = (bf16[64,1024]{1,0:T(8,128)(2,1)S(1)}, bf16[64,1024]{1,0:T(8,128)(2,1)S(1)}, u32[]{:S(2)}, u32[]{:S(2)}) collective-permute-start(bf16[64,1024]{1,0:T(8,128)(2,1)S(1)} %bitcast.99), channel_id=1, source_target_pairs={{12,0},{16,4},{20,8},{24,12},{28,16},{32,20},{36,24},{40,28},{44,3... | collective-permute-start | bytes 393224 | tf_op jit(solution)/shard_map/ppermute | solution.py:16
  49.8 20.0 %collective-permute-start.2 = (bf16[64,1024]{1,0:T(8,128)(2,1)S(1)}, bf16[64,1024]{1,0:T(8,128)(2,1)S(1)}, u32[]{:S(2)}, u32[]{:S(2)}) collective-permute-start(bf16[64,1024]{1,0:T(8,128)(2,1)S(1)} %bitcast.98), channel_id=1, source_target_pairs={{8,0},{12,4},{16,8},{20,12},{24,16},{28,20},{32,24},{36,28},{40,32... | collective-permute-start | bytes 393224 | tf_op jit(solution)/shard_map/ppermute | solution.py:16
  57.8 12.1 %collective-permute-start.3 = (bf16[64,1024]{1,0:T(8,128)(2,1)S(1)}, bf16[64,1024]{1,0:T(8,128)(2,1)S(1)}, u32[]{:S(2)}, u32[]{:S(2)}) collective-permute-start(bf16[64,1024]{1,0:T(8,128)(2,1)S(1)} %bitcast.97), channel_id=1, source_target_pairs={{4,0},{8,4},{12,8},{16,12},{20,16},{24,20},{28,24},{32,28},{36,32}... | collective-permute-start | bytes 393224 | tf_op jit(solution)/shard_map/ppermute | solution.py:16
  59.7 10.3 %collective-permute-start.4 = (bf16[64,1024]{1,0:T(8,128)(2,1)S(1)}, bf16[64,1024]{1,0:T(8,128)(2,1)S(1)}, u32[]{:S(2)}, u32[]{:S(2)}) collective-permute-start(bf16[64,1024]{1,0:T(8,128)(2,1)S(1)} %bitcast.96), channel_id=1, source_target_pairs={{0,4},{4,8},{8,12},{12,16},{16,20},{20,24},{24,28},{28,32},{32,36}... | collective-permute-start | bytes 393224 | tf_op jit(solution)/shard_map/ppermute | solution.py:16
  65.9 8.5 %collective-permute-start.5 = (bf16[64,1024]{1,0:T(8,128)(2,1)S(1)}, bf16[64,1024]{1,0:T(8,128)(2,1)S(1)}, u32[]{:S(2)}, u32[]{:S(2)}) collective-permute-start(bf16[64,1024]{1,0:T(8,128)(2,1)S(1)} %bitcast.95), channel_id=1, source_target_pairs={{0,8},{4,12},{8,16},{12,20},{16,24},{20,28},{24,32},{28,36},{32,40... | collective-permute-start | bytes 393224 | tf_op jit(solution)/shard_map/ppermute | solution.py:16
  67.9 9.0 %collective-permute-start.6 = (bf16[64,1024]{1,0:T(8,128)(2,1)S(1)}, bf16[64,1024]{1,0:T(8,128)(2,1)S(1)}, u32[]{:S(2)}, u32[]{:S(2)}) collective-permute-start(bf16[64,1024]{1,0:T(8,128)(2,1)S(1)} %bitcast.94), channel_id=1, source_target_pairs={{0,12},{4,16},{8,20},{12,24},{16,28},{20,32},{24,36},{28,40},{32,4... | collective-permute-start | bytes 393224 | tf_op jit(solution)/shard_map/ppermute | solution.py:16
  78.7 3.4 %copy-start = (f32[2,256,4096]{2,1,0:T(8,128)}, f32[2,256,4096]{2,1,0:T(8,128)S(1)}, u32[]{:S(2)}) copy-start(f32[2,256,4096]{2,1,0:T(8,128)S(1)} %fusion.14) | copy-start | bytes 25165828
  82.1 15.5 %collective-permute-start = (bf16[256,1024]{1,0:T(8,128)(2,1)S(1)}, bf16[256,1024]{1,0:T(8,128)(2,1)S(1)}, u32[]{:S(2)}, u32[]{:S(2)}) collective-permute-start(bf16[256,1024]{1,0:T(8,128)(2,1)S(1)} %get-tuple-element.215), channel_id=1, source_target_pairs={{240,0},{244,4},{248,8},{252,12},{0,16},{4,20},{8,24},{12,28},{16,... | collective-permute-start | bytes 1572872 | tf_op jit(solution)/shard_map/while/body/eval_jaxpr/ppermute | solution.py:22
  98.9 14.6 %collective-permute-start = (bf16[256,1024]{1,0:T(8,128)(2,1)S(1)}, bf16[256,1024]{1,0:T(8,128)(2,1)S(1)}, u32[]{:S(2)}, u32[]{:S(2)}) collective-permute-start(bf16[256,1024]{1,0:T(8,128)(2,1)S(1)} %get-tuple-element.215), channel_id=1, source_target_pairs={{240,0},{244,4},{248,8},{252,12},{0,16},{4,20},{8,24},{12,28},{16,... | collective-permute-start | bytes 1572872 | tf_op jit(solution)/shard_map/while/body/eval_jaxpr/ppermute | solution.py:22
  114.8 13.7 %collective-permute-start = (bf16[256,1024]{1,0:T(8,128)(2,1)S(1)}, bf16[256,1024]{1,0:T(8,128)(2,1)S(1)}, u32[]{:S(2)}, u32[]{:S(2)}) collective-permute-start(bf16[256,1024]{1,0:T(8,128)(2,1)S(1)} %get-tuple-element.215), channel_id=1, source_target_pairs={{240,0},{244,4},{248,8},{252,12},{0,16},{4,20},{8,24},{12,28},{16,... | collective-permute-start | bytes 1572872 | tf_op jit(solution)/shard_map/while/body/eval_jaxpr/ppermute | solution.py:22
  129.8 12.7 %collective-permute-start = (bf16[256,1024]{1,0:T(8,128)(2,1)S(1)}, bf16[256,1024]{1,0:T(8,128)(2,1)S(1)}, u32[]{:S(2)}, u32[]{:S(2)}) collective-permute-start(bf16[256,1024]{1,0:T(8,128)(2,1)S(1)} %get-tuple-element.215), channel_id=1, source_target_pairs={{240,0},{244,4},{248,8},{252,12},{0,16},{4,20},{8,24},{12,28},{16,... | collective-permute-start | bytes 1572872 | tf_op jit(solution)/shard_map/while/body/eval_jaxpr/ppermute | solution.py:22
  143.9 11.8 %collective-permute-start = (bf16[256,1024]{1,0:T(8,128)(2,1)S(1)}, bf16[256,1024]{1,0:T(8,128)(2,1)S(1)}, u32[]{:S(2)}, u32[]{:S(2)}) collective-permute-start(bf16[256,1024]{1,0:T(8,128)(2,1)S(1)} %get-tuple-element.215), channel_id=1, source_target_pairs={{240,0},{244,4},{248,8},{252,12},{0,16},{4,20},{8,24},{12,28},{16,... | collective-permute-start | bytes 1572872 | tf_op jit(solution)/shard_map/while/body/eval_jaxpr/ppermute | solution.py:22
  157.0 11.4 %collective-permute-start = (bf16[256,1024]{1,0:T(8,128)(2,1)S(1)}, bf16[256,1024]{1,0:T(8,128)(2,1)S(1)}, u32[]{:S(2)}, u32[]{:S(2)}) collective-permute-start(bf16[256,1024]{1,0:T(8,128)(2,1)S(1)} %get-tuple-element.215), channel_id=1, source_target_pairs={{240,0},{244,4},{248,8},{252,12},{0,16},{4,20},{8,24},{12,28},{16,... | collective-permute-start | bytes 1572872 | tf_op jit(solution)/shard_map/while/body/eval_jaxpr/ppermute | solution.py:22
  169.7 12.5 %collective-permute-start = (bf16[256,1024]{1,0:T(8,128)(2,1)S(1)}, bf16[256,1024]{1,0:T(8,128)(2,1)S(1)}, u32[]{:S(2)}, u32[]{:S(2)}) collective-permute-start(bf16[256,1024]{1,0:T(8,128)(2,1)S(1)} %get-tuple-element.215), channel_id=1, source_target_pairs={{240,0},{244,4},{248,8},{252,12},{0,16},{4,20},{8,24},{12,28},{16,... | collective-permute-start | bytes 1572872 | tf_op jit(solution)/shard_map/while/body/eval_jaxpr/ppermute | solution.py:22
  183.5 13.6 %collective-permute-start = (bf16[256,1024]{1,0:T(8,128)(2,1)S(1)}, bf16[256,1024]{1,0:T(8,128)(2,1)S(1)}, u32[]{:S(2)}, u32[]{:S(2)}) collective-permute-start(bf16[256,1024]{1,0:T(8,128)(2,1)S(1)} %get-tuple-element.215), channel_id=1, source_target_pairs={{240,0},{244,4},{248,8},{252,12},{0,16},{4,20},{8,24},{12,28},{16,... | collective-permute-start | bytes 1572872 | tf_op jit(solution)/shard_map/while/body/eval_jaxpr/ppermute | solution.py:22
  198.4 14.6 %collective-permute-start = (bf16[256,1024]{1,0:T(8,128)(2,1)S(1)}, bf16[256,1024]{1,0:T(8,128)(2,1)S(1)}, u32[]{:S(2)}, u32[]{:S(2)}) collective-permute-start(bf16[256,1024]{1,0:T(8,128)(2,1)S(1)} %get-tuple-element.215), channel_id=1, source_target_pairs={{240,0},{244,4},{248,8},{252,12},{0,16},{4,20},{8,24},{12,28},{16,... | collective-permute-start | bytes 1572872 | tf_op jit(solution)/shard_map/while/body/eval_jaxpr/ppermute | solution.py:22
  214.3 15.8 %collective-permute-start = (bf16[256,1024]{1,0:T(8,128)(2,1)S(1)}, bf16[256,1024]{1,0:T(8,128)(2,1)S(1)}, u32[]{:S(2)}, u32[]{:S(2)}) collective-permute-start(bf16[256,1024]{1,0:T(8,128)(2,1)S(1)} %get-tuple-element.215), channel_id=1, source_target_pairs={{240,0},{244,4},{248,8},{252,12},{0,16},{4,20},{8,24},{12,28},{16,... | collective-permute-start | bytes 1572872 | tf_op jit(solution)/shard_map/while/body/eval_jaxpr/ppermute | solution.py:22
  231.4 16.9 %collective-permute-start = (bf16[256,1024]{1,0:T(8,128)(2,1)S(1)}, bf16[256,1024]{1,0:T(8,128)(2,1)S(1)}, u32[]{:S(2)}, u32[]{:S(2)}) collective-permute-start(bf16[256,1024]{1,0:T(8,128)(2,1)S(1)} %get-tuple-element.215), channel_id=1, source_target_pairs={{240,0},{244,4},{248,8},{252,12},{0,16},{4,20},{8,24},{12,28},{16,... | collective-permute-start | bytes 1572872 | tf_op jit(solution)/shard_map/while/body/eval_jaxpr/ppermute | solution.py:22
  249.6 16.1 %collective-permute-start = (bf16[256,1024]{1,0:T(8,128)(2,1)S(1)}, bf16[256,1024]{1,0:T(8,128)(2,1)S(1)}, u32[]{:S(2)}, u32[]{:S(2)}) collective-permute-start(bf16[256,1024]{1,0:T(8,128)(2,1)S(1)} %get-tuple-element.215), channel_id=1, source_target_pairs={{240,0},{244,4},{248,8},{252,12},{0,16},{4,20},{8,24},{12,28},{16,... | collective-permute-start | bytes 1572872 | tf_op jit(solution)/shard_map/while/body/eval_jaxpr/ppermute | solution.py:22
  267.0 15.2 %collective-permute-start = (bf16[256,1024]{1,0:T(8,128)(2,1)S(1)}, bf16[256,1024]{1,0:T(8,128)(2,1)S(1)}, u32[]{:S(2)}, u32[]{:S(2)}) collective-permute-start(bf16[256,1024]{1,0:T(8,128)(2,1)S(1)} %get-tuple-element.215), channel_id=1, source_target_pairs={{240,0},{244,4},{248,8},{252,12},{0,16},{4,20},{8,24},{12,28},{16,... | collective-permute-start | bytes 1572872 | tf_op jit(solution)/shard_map/while/body/eval_jaxpr/ppermute | solution.py:22
  283.5 14.3 %collective-permute-start = (bf16[256,1024]{1,0:T(8,128)(2,1)S(1)}, bf16[256,1024]{1,0:T(8,128)(2,1)S(1)}, u32[]{:S(2)}, u32[]{:S(2)}) collective-permute-start(bf16[256,1024]{1,0:T(8,128)(2,1)S(1)} %get-tuple-element.215), channel_id=1, source_target_pairs={{240,0},{244,4},{248,8},{252,12},{0,16},{4,20},{8,24},{12,28},{16,... | collective-permute-start | bytes 1572872 | tf_op jit(solution)/shard_map/while/body/eval_jaxpr/ppermute | solution.py:22
  299.1 11.3 %collective-permute-start = (bf16[256,1024]{1,0:T(8,128)(2,1)S(1)}, bf16[256,1024]{1,0:T(8,128)(2,1)S(1)}, u32[]{:S(2)}, u32[]{:S(2)}) collective-permute-start(bf16[256,1024]{1,0:T(8,128)(2,1)S(1)} %get-tuple-element.215), channel_id=1, source_target_pairs={{240,0},{244,4},{248,8},{252,12},{0,16},{4,20},{8,24},{12,28},{16,... | collective-permute-start | bytes 1572872 | tf_op jit(solution)/shard_map/while/body/eval_jaxpr/ppermute | solution.py:22
Sparse Core Ops, SparseCore 0:
  9.2 27.6 all-gather.1
where the time goes:
time: 319 us
  waiting for transfers between devices  243 us (76%)
  matrix products  22.4 us (7%)
  starting transfers between devices  22.2 us (7%)
  between operations  13.8 us (4%)
  local copies, waits for them, and re-layouts  11.1 us (3%)
  other arithmetic  5.64 us (2%)
    ppermute x15, waiting for transfers between devices, from_behind(): return lax.ppermute(block, axis, route)  210 us
    all_gather x1, waiting for transfers between devices, local(): lax.all_gather(samples, 'team', axis=0, tiled=True)  26 us
    ppermute x6, starting transfers between devices, shifted(): return lax.ppermute(array, axis, pairs)  22.2 us
    dot_general x16, matrix products, place_tile(): jnp.einsum('crk,pk->crp', local_pair, partner, preferred_element_type=jnp...  19.7 us
    ppermute x6, waiting for transfers between devices, shifted(): return lax.ppermute(array, axis, pairs)  6.8 us
  transfers between devices with their start and end apart: 22, of which 18 were waited for; matrix products, arithmetic and copies ran while one was open for 1% of the time, Pallas kernels for 0%

commit v1 on v0

--- a/solution.py
+++ b/solution.py
@@ -80,9 +80,12 @@
     bin_range = jnp.arange(bin_groups, dtype=jnp.int32)
     avg_range = jnp.arange(AVG, dtype=jnp.int32)
     own_channels = (bin_range[:, None] * team_size + member) * AVG + avg_range[None, :]
-    spectra = filter_bank(lax.all_gather(samples, "team", axis=0, tiled=True), own_channels[None])[
-        :, 0
-    ]
+    spectra = filter_bank(
+        jnp.concatenate(
+            lax.all_to_all(jnp.stack([samples] * lax.axis_size("team")), "team", 0, 0), axis=0
+        ),
+        own_channels[None],
+    )[:, 0]
     packed_all = apply_gains(spectra, input_gains)
     width_k = packed_all.shape[2]
     own_part = lax.dynamic_index_in_dim(packed_all, bin_slot, 0, keepdims=False)

time: 319 us -> 303 us (0.950)
  between operations: 13.8 us -> 0.45 us
  waiting for transfers between devices: 243 us -> 232 us
  starting transfers between devices: 22.2 us -> 28.2 us
    all_gather x1 -> x0, waiting for transfers between devices: 26 us -> none  [local(): lax.all_gather(samples, 'team', axis=0, tiled=True)]
    all_to_all x0 -> x1, waiting for transfers between devices: none -> 18.2 us  [local(): lax.all_to_all(jnp.stack([samples] * lax.axis_size('team')), 'team', 0, 0)]
    all_to_all x0 -> x1, starting transfers between devices: none -> 4.34 us  [local(): lax.all_to_all(jnp.stack([samples] * lax.axis_size('team')), 'team', 0, 0)]
where the time goes in v1:
time: 303 us; the launch traced here: 301 us
  waiting for transfers between devices  232 us (77%)
  starting transfers between devices  28.2 us (9%)
  matrix products  22.4 us (7%)
  local copies, waits for them, and re-layouts  12.4 us (4%)
  other arithmetic  5.67 us (2%)
    ppermute x15, waiting for transfers between devices, from_behind(): return lax.ppermute(block, axis, route)  208 us
    ppermute x6, starting transfers between devices, shifted(): return lax.ppermute(array, axis, pairs)  23.8 us
    dot_general x16, matrix products, place_tile(): jnp.einsum('crk,pk->crp', local_pair, partner, preferred_element_type=jnp...  19.7 us
    all_to_all x1, waiting for transfers between devices, local(): lax.all_to_all(jnp.stack([samples] * lax.axis_size('team')), 'team', 0, 0)  18.2 us
    ppermute x6, waiting for transfers between devices, shifted(): return lax.ppermute(array, axis, pairs)  6.2 us
  transfers between devices with their start and end apart: 22, of which 18 were waited for; matrix products, arithmetic and copies ran while one was open for 1% of the time, Pallas kernels for 0%

profile of v1, /device:TPU:26, one launch (start us, length us, event | category | flops | bytes accessed | tf_op | source)
XLA Modules:
  0.0 301.3 jit_solution(15333697400798107531)
XLA Ops:
  0.0 2.2 stack.8
  2.2 4.3 %all-to-all-start = ((bf16[4,16,11776]{2,1,0:T(8,128)(2,1)}), bf16[4,16,11776]{2,1,0:T(8,128)(2,1)}, u32[]{:S(2)}, u32[]{:S(2)}) async-start(bf16[4,16,11776]{2,1,0:T(8,128)(2,1)} %stack.8), calls=%async_computation | async-start | bytes 3014656 | tf_op jit(solution)/shard_map/all_to_all | solution.py:85
  7.6 1.8 fusion.26
  9.3 18.2 %all-to-all-done = bf16[4,16,11776]{2,1,0:T(8,128)(2,1)} async-done(((bf16[4,16,11776]{2,1,0:T(8,128)(2,1)}), bf16[4,16,11776]{2,1,0:T(8,128)(2,1)}, u32[]{:S(2)}, u32[]{:S(2)}) %all-to-all-start) | async-done | bytes 1507360 | tf_op jit(solution)/shard_map/all_to_all | solution.py:85
  27.5 2.7 reshape.163
  30.2 2.8 fusion.2
  33.0 2.7 fusion.11
  38.1 2.1 collective-permute-start.1
  40.2 9.8 %collective-permute-start.2 = (bf16[64,1024]{1,0:T(8,128)(2,1)S(1)}, bf16[64,1024]{1,0:T(8,128)(2,1)S(1)}, u32[]{:S(2)}, u32[]{:S(2)}) collective-permute-start(bf16[64,1024]{1,0:T(8,128)(2,1)S(1)} %bitcast.98), channel_id=1, source_target_pairs={{8,0},{12,4},{16,8},{20,12},{24,16},{28,20},{32,24},{36,28},{40,32... | collective-permute-start | bytes 393224 | tf_op jit(solution)/shard_map/ppermute | solution.py:16
  50.0 1.9 collective-permute-start.3
  51.9 6.0 %collective-permute-start.4 = (bf16[64,1024]{1,0:T(8,128)(2,1)S(1)}, bf16[64,1024]{1,0:T(8,128)(2,1)S(1)}, u32[]{:S(2)}, u32[]{:S(2)}) collective-permute-start(bf16[64,1024]{1,0:T(8,128)(2,1)S(1)} %bitcast.96), channel_id=1, source_target_pairs={{0,4},{4,8},{8,12},{12,16},{16,20},{20,24},{24,28},{28,32},{32,36}... | collective-permute-start | bytes 393224 | tf_op jit(solution)/shard_map/ppermute | solution.py:16
  58.1 2.0 collective-permute-start.5
  60.2 1.9 collective-permute-start.6
  62.4 4.2 %collective-permute-done.5 = bf16[64,1024]{1,0:T(8,128)(2,1)S(1)} collective-permute-done((bf16[64,1024]{1,0:T(8,128)(2,1)S(1)}, bf16[64,1024]{1,0:T(8,128)(2,1)S(1)}, u32[]{:S(2)}, u32[]{:S(2)}) %collective-permute-start.5) | collective-permute-done | bytes 131104 | tf_op jit(solution)/shard_map/ppermute | solution.py:16
  66.6 2.0 collective-permute-done.6
  70.4 3.4 %copy-done = f32[2,256,4096]{2,1,0:T(8,128)} copy-done((f32[2,256,4096]{2,1,0:T(8,128)}, f32[2,256,4096]{2,1,0:T(8,128)S(1)}, u32[]{:S(2)}) %copy-start) | copy-done | bytes 8388632
  73.8 227.5 %while.17 = (s32[]{:T(128)}, bf16[256,1024]{1,0:T(8,128)(2,1)S(1)}, f32[2,256,4096]{2,1,0:T(8,128)}, bf16[2,256,1024]{2,1,0:T(8,128)(2,1)S(1)}, s32[]{:T(128)}, ...) while((s32[]{:T(128)}, bf16[256,1024]{1,0:T(8,128)(2,1)S(1)}, ...), condition=%wide.region_1.2_spmd, body=%wide.region_0.1_spmd.sunk | while | flops 268566560 | bytes 5243200 | solution.py:130
  73.8 14.9 %collective-permute-done = bf16[256,1024]{1,0:T(8,128)(2,1)S(1)} collective-permute-done((bf16[256,1024]{1,0:T(8,128)(2,1)S(1)}, bf16[256,1024]{1,0:T(8,128)(2,1)S(1)}, u32[]{:S(2)}, u32[]{:S(2)}) %collective-permute-start) | collective-permute-done | bytes 524320 | tf_op jit(solution)/shard_map/while/body/eval_jaxpr/ppermute | solution.py:22
  90.1 14.0 %collective-permute-done = bf16[256,1024]{1,0:T(8,128)(2,1)S(1)} collective-permute-done((bf16[256,1024]{1,0:T(8,128)(2,1)S(1)}, bf16[256,1024]{1,0:T(8,128)(2,1)S(1)}, u32[]{:S(2)}, u32[]{:S(2)}) %collective-permute-start) | collective-permute-done | bytes 524320 | tf_op jit(solution)/shard_map/while/body/eval_jaxpr/ppermute | solution.py:22
  105.4 13.1 %collective-permute-done = bf16[256,1024]{1,0:T(8,128)(2,1)S(1)} collective-permute-done((bf16[256,1024]{1,0:T(8,128)(2,1)S(1)}, bf16[256,1024]{1,0:T(8,128)(2,1)S(1)}, u32[]{:S(2)}, u32[]{:S(2)}) %collective-permute-start) | collective-permute-done | bytes 524320 | tf_op jit(solution)/shard_map/while/body/eval_jaxpr/ppermute | solution.py:22
  119.8 12.2 %collective-permute-done = bf16[256,1024]{1,0:T(8,128)(2,1)S(1)} collective-permute-done((bf16[256,1024]{1,0:T(8,128)(2,1)S(1)}, bf16[256,1024]{1,0:T(8,128)(2,1)S(1)}, u32[]{:S(2)}, u32[]{:S(2)}) %collective-permute-start) | collective-permute-done | bytes 524320 | tf_op jit(solution)/shard_map/while/body/eval_jaxpr/ppermute | solution.py:22
  133.3 11.3 %collective-permute-done = bf16[256,1024]{1,0:T(8,128)(2,1)S(1)} collective-permute-done((bf16[256,1024]{1,0:T(8,128)(2,1)S(1)}, bf16[256,1024]{1,0:T(8,128)(2,1)S(1)}, u32[]{:S(2)}, u32[]{:S(2)}) %collective-permute-start) | collective-permute-done | bytes 524320 | tf_op jit(solution)/shard_map/while/body/eval_jaxpr/ppermute | solution.py:22
  145.9 12.2 %collective-permute-done = bf16[256,1024]{1,0:T(8,128)(2,1)S(1)} collective-permute-done((bf16[256,1024]{1,0:T(8,128)(2,1)S(1)}, bf16[256,1024]{1,0:T(8,128)(2,1)S(1)}, u32[]{:S(2)}, u32[]{:S(2)}) %collective-permute-start) | collective-permute-done | bytes 524320 | tf_op jit(solution)/shard_map/while/body/eval_jaxpr/ppermute | solution.py:22
  159.4 13.3 %collective-permute-done = bf16[256,1024]{1,0:T(8,128)(2,1)S(1)} collective-permute-done((bf16[256,1024]{1,0:T(8,128)(2,1)S(1)}, bf16[256,1024]{1,0:T(8,128)(2,1)S(1)}, u32[]{:S(2)}, u32[]{:S(2)}) %collective-permute-start) | collective-permute-done | bytes 524320 | tf_op jit(solution)/shard_map/while/body/eval_jaxpr/ppermute | solution.py:22
  174.0 14.3 %collective-permute-done = bf16[256,1024]{1,0:T(8,128)(2,1)S(1)} collective-permute-done((bf16[256,1024]{1,0:T(8,128)(2,1)S(1)}, bf16[256,1024]{1,0:T(8,128)(2,1)S(1)}, u32[]{:S(2)}, u32[]{:S(2)}) %collective-permute-start) | collective-permute-done | bytes 524320 | tf_op jit(solution)/shard_map/while/body/eval_jaxpr/ppermute | solution.py:22
  189.7 15.4 %collective-permute-done = bf16[256,1024]{1,0:T(8,128)(2,1)S(1)} collective-permute-done((bf16[256,1024]{1,0:T(8,128)(2,1)S(1)}, bf16[256,1024]{1,0:T(8,128)(2,1)S(1)}, u32[]{:S(2)}, u32[]{:S(2)}) %collective-permute-start) | collective-permute-done | bytes 524320 | tf_op jit(solution)/shard_map/while/body/eval_jaxpr/ppermute | solution.py:22
  206.4 16.6 %collective-permute-done = bf16[256,1024]{1,0:T(8,128)(2,1)S(1)} collective-permute-done((bf16[256,1024]{1,0:T(8,128)(2,1)S(1)}, bf16[256,1024]{1,0:T(8,128)(2,1)S(1)}, u32[]{:S(2)}, u32[]{:S(2)}) %collective-permute-start) | collective-permute-done | bytes 524320 | tf_op jit(solution)/shard_map/while/body/eval_jaxpr/ppermute | solution.py:22
  224.3 16.1 %collective-permute-done = bf16[256,1024]{1,0:T(8,128)(2,1)S(1)} collective-permute-done((bf16[256,1024]{1,0:T(8,128)(2,1)S(1)}, bf16[256,1024]{1,0:T(8,128)(2,1)S(1)}, u32[]{:S(2)}, u32[]{:S(2)}) %collective-permute-start) | collective-permute-done | bytes 524320 | tf_op jit(solution)/shard_map/while/body/eval_jaxpr/ppermute | solution.py:22
  241.7 15.2 %collective-permute-done = bf16[256,1024]{1,0:T(8,128)(2,1)S(1)} collective-permute-done((bf16[256,1024]{1,0:T(8,128)(2,1)S(1)}, bf16[256,1024]{1,0:T(8,128)(2,1)S(1)}, u32[]{:S(2)}, u32[]{:S(2)}) %collective-permute-start) | collective-permute-done | bytes 524320 | tf_op jit(solution)/shard_map/while/body/eval_jaxpr/ppermute | solution.py:22
  258.3 14.3 %collective-permute-done = bf16[256,1024]{1,0:T(8,128)(2,1)S(1)} collective-permute-done((bf16[256,1024]{1,0:T(8,128)(2,1)S(1)}, bf16[256,1024]{1,0:T(8,128)(2,1)S(1)}, u32[]{:S(2)}, u32[]{:S(2)}) %collective-permute-start) | collective-permute-done | bytes 524320 | tf_op jit(solution)/shard_map/while/body/eval_jaxpr/ppermute | solution.py:22
  274.0 13.4 %collective-permute-done = bf16[256,1024]{1,0:T(8,128)(2,1)S(1)} collective-permute-done((bf16[256,1024]{1,0:T(8,128)(2,1)S(1)}, bf16[256,1024]{1,0:T(8,128)(2,1)S(1)}, u32[]{:S(2)}, u32[]{:S(2)}) %collective-permute-start) | collective-permute-done | bytes 524320 | tf_op jit(solution)/shard_map/while/body/eval_jaxpr/ppermute | solution.py:22
  288.7 11.3 %collective-permute-done = bf16[256,1024]{1,0:T(8,128)(2,1)S(1)} collective-permute-done((bf16[256,1024]{1,0:T(8,128)(2,1)S(1)}, bf16[256,1024]{1,0:T(8,128)(2,1)S(1)}, u32[]{:S(2)}, u32[]{:S(2)}) %collective-permute-start) | collective-permute-done | bytes 524320 | tf_op jit(solution)/shard_map/while/body/eval_jaxpr/ppermute | solution.py:22
  (91 shorter events, 25.0 us)
Async XLA Ops:
  0.0 7.6 %copy-start.2 = (f32[2,64,4,32]{1,3,2,0:T(8,128)S(1)}, f32[2,64,4,32]{1,3,2,0:T(8,128)}, u32[]{:S(2)}) copy-start(f32[2,64,4,32]{1,3,2,0:T(8,128)} %param.5) | copy-start | bytes 196612
  2.2 25.3 %all-to-all-start = ((bf16[4,16,11776]{2,1,0:T(8,128)(2,1)}), bf16[4,16,11776]{2,1,0:T(8,128)(2,1)}, u32[]{:S(2)}, u32[]{:S(2)}) async-start(bf16[4,16,11776]{2,1,0:T(8,128)(2,1)} %stack.8), calls=%async_computation | async-start | bytes 3014656 | tf_op jit(solution)/shard_map/all_to_all | solution.py:85
  30.2 2.8 copy-start.1
  38.1 22.0 %collective-permute-start.1 = (bf16[64,1024]{1,0:T(8,128)(2,1)S(1)}, bf16[64,1024]{1,0:T(8,128)(2,1)S(1)}, u32[]{:S(2)}, u32[]{:S(2)}) collective-permute-start(bf16[64,1024]{1,0:T(8,128)(2,1)S(1)} %bitcast.99), channel_id=1, source_target_pairs={{12,0},{16,4},{20,8},{24,12},{28,16},{32,20},{36,24},{40,28},{44,3... | collective-permute-start | bytes 393224 | tf_op jit(solution)/shard_map/ppermute | solution.py:16
  40.2 21.9 %collective-permute-start.2 = (bf16[64,1024]{1,0:T(8,128)(2,1)S(1)}, bf16[64,1024]{1,0:T(8,128)(2,1)S(1)}, u32[]{:S(2)}, u32[]{:S(2)}) collective-permute-start(bf16[64,1024]{1,0:T(8,128)(2,1)S(1)} %bitcast.98), channel_id=1, source_target_pairs={{8,0},{12,4},{16,8},{20,12},{24,16},{28,20},{32,24},{36,28},{40,32... | collective-permute-start | bytes 393224 | tf_op jit(solution)/shard_map/ppermute | solution.py:16
  50.0 12.2 %collective-permute-start.3 = (bf16[64,1024]{1,0:T(8,128)(2,1)S(1)}, bf16[64,1024]{1,0:T(8,128)(2,1)S(1)}, u32[]{:S(2)}, u32[]{:S(2)}) collective-permute-start(bf16[64,1024]{1,0:T(8,128)(2,1)S(1)} %bitcast.97), channel_id=1, source_target_pairs={{4,0},{8,4},{12,8},{16,12},{20,16},{24,20},{28,24},{32,28},{36,32}... | collective-permute-start | bytes 393224 | tf_op jit(solution)/shard_map/ppermute | solution.py:16
  51.9 10.4 %collective-permute-start.4 = (bf16[64,1024]{1,0:T(8,128)(2,1)S(1)}, bf16[64,1024]{1,0:T(8,128)(2,1)S(1)}, u32[]{:S(2)}, u32[]{:S(2)}) collective-permute-start(bf16[64,1024]{1,0:T(8,128)(2,1)S(1)} %bitcast.96), channel_id=1, source_target_pairs={{0,4},{4,8},{8,12},{12,16},{16,20},{20,24},{24,28},{28,32},{32,36}... | collective-permute-start | bytes 393224 | tf_op jit(solution)/shard_map/ppermute | solution.py:16
  58.1 8.5 %collective-permute-start.5 = (bf16[64,1024]{1,0:T(8,128)(2,1)S(1)}, bf16[64,1024]{1,0:T(8,128)(2,1)S(1)}, u32[]{:S(2)}, u32[]{:S(2)}) collective-permute-start(bf16[64,1024]{1,0:T(8,128)(2,1)S(1)} %bitcast.95), channel_id=1, source_target_pairs={{0,8},{4,12},{8,16},{12,20},{16,24},{20,28},{24,32},{28,36},{32,40... | collective-permute-start | bytes 393224 | tf_op jit(solution)/shard_map/ppermute | solution.py:16
  60.2 8.4 %collective-permute-start.6 = (bf16[64,1024]{1,0:T(8,128)(2,1)S(1)}, bf16[64,1024]{1,0:T(8,128)(2,1)S(1)}, u32[]{:S(2)}, u32[]{:S(2)}) collective-permute-start(bf16[64,1024]{1,0:T(8,128)(2,1)S(1)} %bitcast.94), channel_id=1, source_target_pairs={{0,12},{4,16},{8,20},{12,24},{16,28},{20,32},{24,36},{28,40},{32,4... | collective-permute-start | bytes 393224 | tf_op jit(solution)/shard_map/ppermute | solution.py:16
  70.4 3.4 %copy-start = (f32[2,256,4096]{2,1,0:T(8,128)}, f32[2,256,4096]{2,1,0:T(8,128)S(1)}, u32[]{:S(2)}) copy-start(f32[2,256,4096]{2,1,0:T(8,128)S(1)} %fusion.14) | copy-start | bytes 25165828
  73.8 14.9 %collective-permute-start = (bf16[256,1024]{1,0:T(8,128)(2,1)S(1)}, bf16[256,1024]{1,0:T(8,128)(2,1)S(1)}, u32[]{:S(2)}, u32[]{:S(2)}) collective-permute-start(bf16[256,1024]{1,0:T(8,128)(2,1)S(1)} %get-tuple-element.215), channel_id=1, source_target_pairs={{240,0},{244,4},{248,8},{252,12},{0,16},{4,20},{8,24},{12,28},{16,... | collective-permute-start | bytes 1572872 | tf_op jit(solution)/shard_map/while/body/eval_jaxpr/ppermute | solution.py:22
  90.1 14.0 %collective-permute-start = (bf16[256,1024]{1,0:T(8,128)(2,1)S(1)}, bf16[256,1024]{1,0:T(8,128)(2,1)S(1)}, u32[]{:S(2)}, u32[]{:S(2)}) collective-permute-start(bf16[256,1024]{1,0:T(8,128)(2,1)S(1)} %get-tuple-element.215), channel_id=1, source_target_pairs={{240,0},{244,4},{248,8},{252,12},{0,16},{4,20},{8,24},{12,28},{16,... | collective-permute-start | bytes 1572872 | tf_op jit(solution)/shard_map/while/body/eval_jaxpr/ppermute | solution.py:22
  105.4 13.1 %collective-permute-start = (bf16[256,1024]{1,0:T(8,128)(2,1)S(1)}, bf16[256,1024]{1,0:T(8,128)(2,1)S(1)}, u32[]{:S(2)}, u32[]{:S(2)}) collective-permute-start(bf16[256,1024]{1,0:T(8,128)(2,1)S(1)} %get-tuple-element.215), channel_id=1, source_target_pairs={{240,0},{244,4},{248,8},{252,12},{0,16},{4,20},{8,24},{12,28},{16,... | collective-permute-start | bytes 1572872 | tf_op jit(solution)/shard_map/while/body/eval_jaxpr/ppermute | solution.py:22
  119.8 12.2 %collective-permute-start = (bf16[256,1024]{1,0:T(8,128)(2,1)S(1)}, bf16[256,1024]{1,0:T(8,128)(2,1)S(1)}, u32[]{:S(2)}, u32[]{:S(2)}) collective-permute-start(bf16[256,1024]{1,0:T(8,128)(2,1)S(1)} %get-tuple-element.215), channel_id=1, source_target_pairs={{240,0},{244,4},{248,8},{252,12},{0,16},{4,20},{8,24},{12,28},{16,... | collective-permute-start | bytes 1572872 | tf_op jit(solution)/shard_map/while/body/eval_jaxpr/ppermute | solution.py:22
  133.3 11.3 %collective-permute-start = (bf16[256,1024]{1,0:T(8,128)(2,1)S(1)}, bf16[256,1024]{1,0:T(8,128)(2,1)S(1)}, u32[]{:S(2)}, u32[]{:S(2)}) collective-permute-start(bf16[256,1024]{1,0:T(8,128)(2,1)S(1)} %get-tuple-element.215), channel_id=1, source_target_pairs={{240,0},{244,4},{248,8},{252,12},{0,16},{4,20},{8,24},{12,28},{16,... | collective-permute-start | bytes 1572872 | tf_op jit(solution)/shard_map/while/body/eval_jaxpr/ppermute | solution.py:22
  145.9 12.2 %collective-permute-start = (bf16[256,1024]{1,0:T(8,128)(2,1)S(1)}, bf16[256,1024]{1,0:T(8,128)(2,1)S(1)}, u32[]{:S(2)}, u32[]{:S(2)}) collective-permute-start(bf16[256,1024]{1,0:T(8,128)(2,1)S(1)} %get-tuple-element.215), channel_id=1, source_target_pairs={{240,0},{244,4},{248,8},{252,12},{0,16},{4,20},{8,24},{12,28},{16,... | collective-permute-start | bytes 1572872 | tf_op jit(solution)/shard_map/while/body/eval_jaxpr/ppermute | solution.py:22
  159.4 13.3 %collective-permute-start = (bf16[256,1024]{1,0:T(8,128)(2,1)S(1)}, bf16[256,1024]{1,0:T(8,128)(2,1)S(1)}, u32[]{:S(2)}, u32[]{:S(2)}) collective-permute-start(bf16[256,1024]{1,0:T(8,128)(2,1)S(1)} %get-tuple-element.215), channel_id=1, source_target_pairs={{240,0},{244,4},{248,8},{252,12},{0,16},{4,20},{8,24},{12,28},{16,... | collective-permute-start | bytes 1572872 | tf_op jit(solution)/shard_map/while/body/eval_jaxpr/ppermute | solution.py:22
  174.0 14.4 %collective-permute-start = (bf16[256,1024]{1,0:T(8,128)(2,1)S(1)}, bf16[256,1024]{1,0:T(8,128)(2,1)S(1)}, u32[]{:S(2)}, u32[]{:S(2)}) collective-permute-start(bf16[256,1024]{1,0:T(8,128)(2,1)S(1)} %get-tuple-element.215), channel_id=1, source_target_pairs={{240,0},{244,4},{248,8},{252,12},{0,16},{4,20},{8,24},{12,28},{16,... | collective-permute-start | bytes 1572872 | tf_op jit(solution)/shard_map/while/body/eval_jaxpr/ppermute | solution.py:22
  189.7 15.4 %collective-permute-start = (bf16[256,1024]{1,0:T(8,128)(2,1)S(1)}, bf16[256,1024]{1,0:T(8,128)(2,1)S(1)}, u32[]{:S(2)}, u32[]{:S(2)}) collective-permute-start(bf16[256,1024]{1,0:T(8,128)(2,1)S(1)} %get-tuple-element.215), channel_id=1, source_target_pairs={{240,0},{244,4},{248,8},{252,12},{0,16},{4,20},{8,24},{12,28},{16,... | collective-permute-start | bytes 1572872 | tf_op jit(solution)/shard_map/while/body/eval_jaxpr/ppermute | solution.py:22
  206.4 16.6 %collective-permute-start = (bf16[256,1024]{1,0:T(8,128)(2,1)S(1)}, bf16[256,1024]{1,0:T(8,128)(2,1)S(1)}, u32[]{:S(2)}, u32[]{:S(2)}) collective-permute-start(bf16[256,1024]{1,0:T(8,128)(2,1)S(1)} %get-tuple-element.215), channel_id=1, source_target_pairs={{240,0},{244,4},{248,8},{252,12},{0,16},{4,20},{8,24},{12,28},{16,... | collective-permute-start | bytes 1572872 | tf_op jit(solution)/shard_map/while/body/eval_jaxpr/ppermute | solution.py:22
  224.3 16.1 %collective-permute-start = (bf16[256,1024]{1,0:T(8,128)(2,1)S(1)}, bf16[256,1024]{1,0:T(8,128)(2,1)S(1)}, u32[]{:S(2)}, u32[]{:S(2)}) collective-permute-start(bf16[256,1024]{1,0:T(8,128)(2,1)S(1)} %get-tuple-element.215), channel_id=1, source_target_pairs={{240,0},{244,4},{248,8},{252,12},{0,16},{4,20},{8,24},{12,28},{16,... | collective-permute-start | bytes 1572872 | tf_op jit(solution)/shard_map/while/body/eval_jaxpr/ppermute | solution.py:22
  241.7 15.3 %collective-permute-start = (bf16[256,1024]{1,0:T(8,128)(2,1)S(1)}, bf16[256,1024]{1,0:T(8,128)(2,1)S(1)}, u32[]{:S(2)}, u32[]{:S(2)}) collective-permute-start(bf16[256,1024]{1,0:T(8,128)(2,1)S(1)} %get-tuple-element.215), channel_id=1, source_target_pairs={{240,0},{244,4},{248,8},{252,12},{0,16},{4,20},{8,24},{12,28},{16,... | collective-permute-start | bytes 1572872 | tf_op jit(solution)/shard_map/while/body/eval_jaxpr/ppermute | solution.py:22
  258.3 14.3 %collective-permute-start = (bf16[256,1024]{1,0:T(8,128)(2,1)S(1)}, bf16[256,1024]{1,0:T(8,128)(2,1)S(1)}, u32[]{:S(2)}, u32[]{:S(2)}) collective-permute-start(bf16[256,1024]{1,0:T(8,128)(2,1)S(1)} %get-tuple-element.215), channel_id=1, source_target_pairs={{240,0},{244,4},{248,8},{252,12},{0,16},{4,20},{8,24},{12,28},{16,... | collective-permute-start | bytes 1572872 | tf_op jit(solution)/shard_map/while/body/eval_jaxpr/ppermute | solution.py:22
  274.0 13.4 %collective-permute-start = (bf16[256,1024]{1,0:T(8,128)(2,1)S(1)}, bf16[256,1024]{1,0:T(8,128)(2,1)S(1)}, u32[]{:S(2)}, u32[]{:S(2)}) collective-permute-start(bf16[256,1024]{1,0:T(8,128)(2,1)S(1)} %get-tuple-element.215), channel_id=1, source_target_pairs={{240,0},{244,4},{248,8},{252,12},{0,16},{4,20},{8,24},{12,28},{16,... | collective-permute-start | bytes 1572872 | tf_op jit(solution)/shard_map/while/body/eval_jaxpr/ppermute | solution.py:22
  288.7 11.3 %collective-permute-start = (bf16[256,1024]{1,0:T(8,128)(2,1)S(1)}, bf16[256,1024]{1,0:T(8,128)(2,1)S(1)}, u32[]{:S(2)}, u32[]{:S(2)}) collective-permute-start(bf16[256,1024]{1,0:T(8,128)(2,1)S(1)} %get-tuple-element.215), channel_id=1, source_target_pairs={{240,0},{244,4},{248,8},{252,12},{0,16},{4,20},{8,24},{12,28},{16,... | collective-permute-start | bytes 1572872 | tf_op jit(solution)/shard_map/while/body/eval_jaxpr/ppermute | solution.py:22
